TPU v7x, 128 devices: a whole 4x4x4 slice. The times are simulated.
128 devices in a mesh: batch: 8 (over x, core), tensor: 16 (over y, z).
Axes of the slice: x: 4, y: 4, z: 4, core: 2. Of those that a mesh axis runs over, the one named last changes fastest.
Arguments:
- tokens: bfloat16 [256, 8192], P('batch'), may hold values from -6 to 6
- row_adapter_index: int32 [256], P('batch'), may hold values from 0 to 31, as said below
- adapter_store_row: int32 [32], replicated, may hold values from 0 to 31, as said below
- lengths: int32 [256], P('batch'), may hold values from 2 to 512, as said below
- query_weight: bfloat16 [8192, 8192], P(None, 'tensor'), may hold values from -0.0625 to 0.0625
- key_weight: bfloat16 [8192, 1024], P(None, 'tensor'), may hold values from -0.0625 to 0.0625
- value_weight: bfloat16 [8192, 1024], P(None, 'tensor'), may hold values from -0.0625 to 0.0625
- output_weight: bfloat16 [8192, 8192], P('tensor'), may hold values from -0.09375 to 0.09375
- adapter_down_weight: bfloat16 [32, 48, 8192], P('batch', None, 'tensor'), may hold values from -0.0625 to 0.0625
- adapter_up_query: bfloat16 [32, 16, 8192], P('batch', None, 'tensor'), may hold values from -1.5 to 1.5
- adapter_up_key: bfloat16 [32, 16, 1024], P('batch', None, 'tensor'), may hold values from -1.5 to 1.5
- adapter_up_value: bfloat16 [32, 16, 1024], P('batch', None, 'tensor'), may hold values from -1.5 to 1.5
- cached_key_rows: bfloat16 [256, 512, 1024], P(('batch', 'tensor')), may hold values from -530 to 530
- cached_value_rows: bfloat16 [256, 512, 1024], P(('batch', 'tensor')), may hold values from -6 to 6
Outputs:
- attn_out: bfloat16 [256, 8192], P('batch', 'tensor')
Inputs may be any that keep to these rules, and one draw needn't show every extreme that they name: A permutation: adapter a lies in row adapter_store_row[a] of the adapter arrays; rows o * 4 to (o + 1) * 4 - 1 lie with batch group o. `row_adapter_index`: of the rows of one batch group, at most 8 have adapters stored with any one batch group, and exactly 8 with some batch group. `lengths`: the first row of each batch group has all 512 positions.
All inputs are finite; a program needn't handle non-finite values.
Results may differ from a plain program's by a relative error of at most 0.035.
Values may be sent and summed in bfloat16 or wider, within the bound.
A program may use at most 64 MiB of HBM per device.

v0:
```python
import math

import jax
import jax.numpy as jnp
from jax import lax
from jax.sharding import PartitionSpec as P

QUERY_HEADS = 64
KEY_VALUE_HEADS = 8
HEAD_WIDTH = 128
ADAPTER_RANK = 16


ADAPTER_SCALE = 0.5
MASKED_SCORE = -1e30


def shrink_terms(inputs, down_rows, select):
    adapter_terms = jnp.einsum("md,kjd->mkj", inputs, down_rows, preferred_element_type=jnp.float32)
    return jnp.sum(jnp.where(select[:, :, None], adapter_terms, 0.0), axis=1)


def expand_terms(summed_terms, up_tables, select):
    scaled_terms = (ADAPTER_SCALE * summed_terms).astype(jnp.bfloat16)
    outputs = []
    for projection_choice in range(3):
        piece_cols = scaled_terms[
            :, projection_choice * ADAPTER_RANK : (projection_choice + 1) * ADAPTER_RANK
        ]
        masked = jnp.where(select[:, :, None], piece_cols[:, None, :], jnp.zeros((), jnp.bfloat16))
        flattened = masked.reshape(masked.shape[0], -1)
        up_weight_table = up_tables[projection_choice]
        product = jnp.dot(
            flattened,
            up_weight_table.reshape(-1, up_weight_table.shape[2]),
            preferred_element_type=jnp.float32,
        )
        outputs.append(product.astype(jnp.bfloat16))
    return outputs


def on_device(
    tokens,
    row_adapter_index,
    adapter_store_row,
    lengths,
    query_weight,
    key_weight,
    value_weight,
    output_weight,
    adapter_down_weight,
    adapter_up_query,
    adapter_up_key,
    adapter_up_value,
    cached_key_rows,
    cached_value_rows,
):
    tensor_rank = lax.axis_index("tensor")
    width_portion = adapter_down_weight.shape[2]
    own_tokens = lax.dynamic_slice_in_dim(tokens, tensor_rank * width_portion, width_portion, 1)
    adapters_all = adapter_store_row.shape[0]
    store_ids = jnp.arange(adapters_all, dtype=jnp.int32)
    slot_rows = jnp.sum(
        jnp.where(row_adapter_index[:, None] == store_ids[None, :], adapter_store_row[None, :], 0),
        axis=1,
    )
    fetched_store = (
        lax.all_gather(adapter_down_weight, "batch", axis=0, tiled=True),
        lax.all_gather(adapter_up_query, "batch", axis=0, tiled=True),
        lax.all_gather(adapter_up_key, "batch", axis=0, tiled=True),
        lax.all_gather(adapter_up_value, "batch", axis=0, tiled=True),
    )
    select = slot_rows[:, None] == store_ids[None, :]
    summed_terms = lax.psum(shrink_terms(own_tokens, fetched_store[0], select), "tensor")
    delta_q, delta_k, delta_v = expand_terms(summed_terms, fetched_store[1:], select)
    query_local = (
        jnp.dot(tokens, query_weight, preferred_element_type=jnp.float32)
        + delta_q.astype(jnp.float32)
    ).astype(jnp.bfloat16)
    key_local = (
        jnp.dot(tokens, key_weight, preferred_element_type=jnp.float32)
        + delta_k.astype(jnp.float32)
    ).astype(jnp.bfloat16)
    value_local = (
        jnp.dot(tokens, value_weight, preferred_element_type=jnp.float32)
        + delta_v.astype(jnp.float32)
    ).astype(jnp.bfloat16)
    queries, keys_new, values_new = (
        lax.all_to_all(query_local, "tensor", split_axis=0, concat_axis=1, tiled=True),
        lax.all_to_all(key_local, "tensor", split_axis=0, concat_axis=1, tiled=True),
        lax.all_to_all(value_local, "tensor", split_axis=0, concat_axis=1, tiled=True),
    )
    rows_here = cached_key_rows.shape[0]
    cache_span = cached_key_rows.shape[1]
    head_group = QUERY_HEADS // KEY_VALUE_HEADS
    score_scale = 1.0 / math.sqrt(HEAD_WIDTH)
    own_lengths = lax.dynamic_slice_in_dim(lengths, tensor_rank * rows_here, rows_here, 0)
    query_heads = queries.reshape(rows_here, KEY_VALUE_HEADS, head_group, HEAD_WIDTH)
    cached_keys = cached_key_rows.reshape(rows_here, cache_span, KEY_VALUE_HEADS, HEAD_WIDTH)
    cached_values = cached_value_rows.reshape(rows_here, cache_span, KEY_VALUE_HEADS, HEAD_WIDTH)
    scores = (
        jnp.einsum("rghd,rpgd->rghp", query_heads, cached_keys, preferred_element_type=jnp.float32)
        * score_scale
    )
    self_scores = (
        jnp.einsum(
            "rghd,rgd->rgh",
            query_heads,
            keys_new.reshape(rows_here, KEY_VALUE_HEADS, HEAD_WIDTH),
            preferred_element_type=jnp.float32,
        )
        * score_scale
    )
    positions = jnp.arange(cache_span, dtype=jnp.int32)
    is_valid = (positions[None, :] < own_lengths[:, None])[:, None, None, :]
    top_score = jnp.maximum(jnp.max(jnp.where(is_valid, scores, MASKED_SCORE), axis=3), self_scores)
    weights = jnp.where(is_valid, jnp.exp(scores - top_score[..., None]), 0.0)
    self_weight = jnp.exp(self_scores - top_score)
    full_total = jnp.sum(weights, axis=3) + self_weight
    numerator = jnp.einsum(
        "rghp,rpgd->rghd",
        weights.astype(jnp.bfloat16),
        cached_values,
        preferred_element_type=jnp.float32,
    )
    rounded_self = lax.optimization_barrier(self_weight.astype(jnp.bfloat16)).astype(jnp.float32)
    numerator = numerator + rounded_self[..., None] * values_new.reshape(
        rows_here, KEY_VALUE_HEADS, 1, HEAD_WIDTH
    ).astype(jnp.float32)
    attended = (
        (numerator / full_total[..., None])
        .astype(jnp.bfloat16)
        .reshape(rows_here, QUERY_HEADS * HEAD_WIDTH)
    )
    head_rows = lax.all_to_all(attended, "tensor", split_axis=1, concat_axis=0, tiled=True)
    partial_out = jnp.dot(head_rows, output_weight, preferred_element_type=jnp.float32)
    return lax.psum_scatter(partial_out, "tensor", scatter_dimension=1, tiled=True).astype(
        jnp.bfloat16
    )


def solution(mesh):
    placed = (
        P("batch", None),
        P("batch"),
        P(),
        P("batch"),
        P(None, "tensor"),
        P(None, "tensor"),
        P(None, "tensor"),
        P("tensor", None),
        P("batch", None, "tensor"),
        P("batch", None, "tensor"),
        P("batch", None, "tensor"),
        P("batch", None, "tensor"),
        P(("batch", "tensor"), None, None),
        P(("batch", "tensor"), None, None),
    )
    return jax.shard_map(
        on_device, mesh=mesh, in_specs=placed, out_specs=P("batch", "tensor"), check_vma=False
    )
```

profile of v0, /device:TPU:0, one launch (start us, length us, event | category | flops | bytes accessed | tf_op | source)
XLA Modules:
  0.0 262.0 jit_solution(11696534463470443802)
XLA Ops:
  6.5 0.7 all-gather.2.cloned.1.call-update
  7.3 0.9 select_reduce_fusion.1
  8.2 0.1 copy.46
  8.3 0.7 dynamic_slice.6
  9.0 13.4 %all_gather.14 = bf16[32,16,64]{2,1,0:T(8,128)(2,1)S(1)} all-gather(bf16[4,16,64]{2,1,0:T(8,128)(2,1)} %param.24), channel_id=1, replica_groups=mesh['batch'=8,'tensor'=16] {'batch'}, dimensions={0}, use_global_device_ids=true | all-gather | bytes 73728 | tf_op jit(solution)/shard_map/all_gather | solution.py:70
  22.4 13.0 %all_gather.15 = bf16[32,16,64]{2,1,0:T(8,128)(2,1)S(1)} all-gather(bf16[4,16,64]{2,1,0:T(8,128)(2,1)} %param.25), channel_id=1, replica_groups=mesh['batch'=8,'tensor'=16] {'batch'}, dimensions={0}, use_global_device_ids=true | all-gather | bytes 73728 | tf_op jit(solution)/shard_map/all_gather | solution.py:71
  35.4 13.3 %all_gather.13 = bf16[32,16,512]{2,1,0:T(8,128)(2,1)S(1)} all-gather(bf16[4,16,512]{2,1,0:T(8,128)(2,1)} %param.23), channel_id=1, replica_groups=mesh['batch'=8,'tensor'=16] {'batch'}, dimensions={0}, use_global_device_ids=true | all-gather | bytes 589824 | tf_op jit(solution)/shard_map/all_gather | solution.py:69
  48.7 2.4 fusion.6
  51.2 75.9 %psum.7 = f32[32,48]{1,0:T(8,128)S(1)} all-reduce(f32[32,48]{1,0:T(8,128)S(1)} %fusion.6), channel_id=1, replica_groups=mesh['batch'=8,'tensor'=16] {'tensor'}, use_global_device_ids=true, to_apply=%region_2.3 | all-reduce | flops 1536 | bytes 12288 | tf_op jit(solution)/shard_map/psum | solution.py:74
  127.3 0.3 fusion.25
  127.6 2.2 fusion.22
  129.9 3.5 %all-to-all-start.1 = ((bf16[16,2,64]{2,1,0:T(2,128)(2,1)}), bf16[16,2,64]{2,1,0:T(2,128)(2,1)S(1)}, u32[]{:S(2)}, u32[]{:S(2)}) async-start(bf16[16,2,64]{2,1,0:T(2,128)(2,1)} %bitcast.4), calls=%async_computation.1 | async-start | bytes 16384 | tf_op jit(solution)/shard_map/all_to_all | solution.py:90
  133.4 0.3 fusion.27
  133.7 2.2 fusion.23
  136.0 0.4 fusion.18
  136.4 4.4 %all-to-all-done.1 = bf16[16,2,64]{2,1,0:T(2,128)(2,1)S(1)} async-done(((bf16[16,2,64]{2,1,0:T(2,128)(2,1)}), bf16[16,2,64]{2,1,0:T(2,128)(2,1)S(1)}, u32[]{:S(2)}, u32[]{:S(2)}) %all-to-all-start.1) | async-done | bytes 4128 | tf_op jit(solution)/shard_map/all_to_all | solution.py:90
  140.8 3.4 %all-to-all-start.2 = ((bf16[16,2,64]{2,1,0:T(2,128)(2,1)}), bf16[16,2,64]{2,1,0:T(2,128)(2,1)S(1)}, u32[]{:S(2)}, u32[]{:S(2)}) async-start(bf16[16,2,64]{2,1,0:T(2,128)(2,1)} %bitcast.9), calls=%async_computation.2 | async-start | bytes 16384 | tf_op jit(solution)/shard_map/all_to_all | solution.py:91
  144.2 4.9 %fusion.16 = bf16[32,512]{1,0:T(8,128)(2,1)S(1)} fusion(f32[32,512]{1,0:T(8,128)S(1)} %fusion.18, bf16[32,8192]{1,0:T(8,128)(2,1)S(1)} %copy-done.1, bf16[8192,512]{1,0:T(8,128)(2,1)} %param.18), kind=kOutput, calls=%fused_computation.13 | convolution fusion | flops 268468224 | bytes 9011200 | tf_op jit(solution)/shard_map/dot_general | solution.py:77
  149.1 0.7 all_to_all.48
  149.8 1.9 all-to-all-done.2
  151.7 5.2 %all-to-all-start = ((bf16[16,2,512]{2,1,0:T(2,128)(2,1)}), bf16[16,2,512]{2,1,0:T(2,128)(2,1)S(1)}, u32[]{:S(2)}, u32[]{:S(2)}) async-start(bf16[16,2,512]{2,1,0:T(2,128)(2,1)} %all_to_all.48), calls=%async_computation | async-start | bytes 65536 | tf_op jit(solution)/shard_map/all_to_all | solution.py:89
  157.0 0.1 reshape.103
  157.2 7.4 %all-to-all-done = bf16[16,2,512]{2,1,0:T(2,128)(2,1)S(1)} async-done(((bf16[16,2,512]{2,1,0:T(2,128)(2,1)}), bf16[16,2,512]{2,1,0:T(2,128)(2,1)S(1)}, u32[]{:S(2)}, u32[]{:S(2)}) %all-to-all-start) | async-done | bytes 32800 | tf_op jit(solution)/shard_map/all_to_all | solution.py:89
  164.6 0.1 fusion.59
  164.7 0.7 select_reduce_fusion
  165.5 0.2 fusion.29
  165.7 0.5 copy-done.2
  166.2 0.5 fusion.19
  166.8 10.7 %all_to_all.64 = bf16[2,16,512]{2,0,1:T(2,128)(2,1)S(1)} all-to-all(bf16[2,16,512]{2,0,1:T(2,128)(2,1)S(1)} %copy.58), channel_id=1, replica_groups=mesh['batch'=8,'tensor'=16] {'tensor'}, dimensions={1} | all-to-all | bytes 65536 | tf_op jit(solution)/shard_map/all_to_all | solution.py:135
  177.5 5.9 %fusion.60 = f32[32,8192]{1,0:T(8,128)} fusion(bf16[32,512]{1,0:T(8,128)(2,1)S(1)} %all_to_all.59, bf16[512,8192]{1,0:T(8,128)(2,1)} %param.21), kind=kOutput, calls=%fused_computation.68 | convolution fusion | flops 268435456 | bytes 9469952 | tf_op jit(solution)/shard_map/dot_general | solution.py:136
  183.5 70.2 %reduce-scatter.2.cloned.1.call-done = f32[32,512]{1,0:T(8,128)} async-done(((f32[32,8192]{1,0:T(8,128)}), f32[32,512]{1,0:T(8,128)}) %reduce-scatter.2.cloned.1.call-update) | async-done | bytes 65552 | tf_op jit(solution)/shard_map/reduce_scatter | solution.py:137
  253.7 1.5 convert_element_type.76
  (28 shorter events, 0.7 us)
Async XLA Ops:
  6.5 158.2 %copy-start = (bf16[2,512,1024]{2,1,0:T(8,128)(2,1)S(1)}, bf16[2,512,1024]{2,1,0:T(8,128)(2,1)}, u32[]{:S(2)}) copy-start(bf16[2,512,1024]{2,1,0:T(8,128)(2,1)} %param.26) | copy-start | bytes 6291460
  6.5 121.1 %copy-start.1 = (bf16[32,8192]{1,0:T(8,128)(2,1)S(1)}, bf16[32,8192]{1,0:T(8,128)(2,1)}, u32[]{:S(2)}) copy-start(bf16[32,8192]{1,0:T(8,128)(2,1)} %param.14) | copy-start | bytes 1572868
  6.5 42.2 %all-gather.2.cloned.1.call-start = ((), (), s32[]{:S(2)}) async-start(), calls=%async_computation.5 | async-start | bytes 1769472 | tf_op jit(solution)/shard_map/all_gather | solution.py:68
  129.9 10.9 %all-to-all-start.1 = ((bf16[16,2,64]{2,1,0:T(2,128)(2,1)}), bf16[16,2,64]{2,1,0:T(2,128)(2,1)S(1)}, u32[]{:S(2)}, u32[]{:S(2)}) async-start(bf16[16,2,64]{2,1,0:T(2,128)(2,1)} %bitcast.4), calls=%async_computation.1 | async-start | bytes 16384 | tf_op jit(solution)/shard_map/all_to_all | solution.py:90
  140.8 10.9 %all-to-all-start.2 = ((bf16[16,2,64]{2,1,0:T(2,128)(2,1)}), bf16[16,2,64]{2,1,0:T(2,128)(2,1)S(1)}, u32[]{:S(2)}, u32[]{:S(2)}) async-start(bf16[16,2,64]{2,1,0:T(2,128)(2,1)} %bitcast.9), calls=%async_computation.2 | async-start | bytes 16384 | tf_op jit(solution)/shard_map/all_to_all | solution.py:91
  151.7 12.8 %all-to-all-start = ((bf16[16,2,512]{2,1,0:T(2,128)(2,1)}), bf16[16,2,512]{2,1,0:T(2,128)(2,1)S(1)}, u32[]{:S(2)}, u32[]{:S(2)}) async-start(bf16[16,2,512]{2,1,0:T(2,128)(2,1)} %all_to_all.48), calls=%async_computation | async-start | bytes 65536 | tf_op jit(solution)/shard_map/all_to_all | solution.py:89
  156.9 96.8 %reduce-scatter.2.cloned.1.call-start = ((), (), s32[]{:S(2)}) async-start(), calls=%async_computation.6 | async-start | bytes 1114112 | tf_op jit(solution)/shard_map/reduce_scatter | solution.py:137
  164.6 1.6 copy-start.2
Sparse Core Ops, SparseCore 0:
  9.0 27.0 all-gather.1
  183.6 70.0 reduce-scatter.1
where the time goes:
time: 263 us; the launch traced here: 262 us
  blocking collectives  126 us (48%)
  waiting for transfers between devices  84.6 us (32%)
  matrix products  20.1 us (8%)
  between operations  13.5 us (5%)
  starting transfers between devices  12.1 us (5%)
  other arithmetic  2.68 us (1%)
    psum x1, blocking collectives, on_device(): lax.psum(shrink_terms(own_tokens, fetched_store[0], select), 'tensor')  75.9 us
    reduce_scatter x1, waiting for transfers between devices, on_device(): lax.psum_scatter(partial_out, 'tensor', scatter_dimension=1, tiled=True)  70.2 us
    all_gather x1, blocking collectives, on_device(): lax.all_gather(adapter_up_key, 'batch', axis=0, tiled=True)  13.4 us
    all_gather x1, blocking collectives, on_device(): lax.all_gather(adapter_up_query, 'batch', axis=0, tiled=True)  13.3 us
    all_gather x1, blocking collectives, on_device(): lax.all_gather(adapter_up_value, 'batch', axis=0, tiled=True)  13 us
    all_to_all x1, blocking collectives, on_device(): lax.all_to_all(attended, 'tensor', split_axis=1, concat_axis=0, tiled=True)  10.7 us
    all_to_all x1, waiting for transfers between devices, on_device(): lax.all_to_all(query_local, 'tensor', split_axis=0, concat_axis=1, tiled=...  7.38 us
    dot_general x1, matrix products, on_device(): jnp.dot(head_rows, output_weight, preferred_element_type=jnp.float32)  5.92 us
  transfers between devices with their start and end apart: 5, of which 4 were waited for; matrix products, arithmetic and copies ran while one was open for 4% of the time, Pallas kernels for 0%

commit v1 on v0

v1 whole, which is shorter than its diff:
```python
import functools
import math

import jax
import jax.numpy as jnp
from jax import lax
from jax.experimental import pallas as pl
from jax.experimental.pallas import tpu as pltpu
from jax.sharding import PartitionSpec as P

HEAD_WIDTH = 128
ADAPTER_SCALE = 0.5
MASKED_SCORE = -1e30
MESH = pl.DeviceIdType.MESH
F32 = jnp.float32
BF16 = jnp.bfloat16

GROUPS = 8
SPLIT = 16
CAP = 8
ROWS = 32
QUERY_CHUNKS = 8
DEPTH = 8192
COLS = 512
SPAN = 512
TRANS_B = (((1,), (1,)), ((), ()))


def iota(shape, dim):
    return lax.broadcasted_iota(jnp.int32, shape, dim)


def dot(a, b):
    return jnp.dot(a, b, preferred_element_type=F32)


def dot_tb(a, b):
    return lax.dot_general(a, b, TRANS_B, preferred_element_type=F32)


def kernel(
    index_ref,
    store_ref,
    length_ref,
    tokens_hbm,
    query_hbm,
    key_hbm,
    value_hbm,
    output_hbm,
    down_hbm,
    up_query_hbm,
    up_key_hbm,
    up_value_hbm,
    cache_key_hbm,
    cache_value_hbm,
    out_ref,
    tokens,
    query_w,
    kv_w,
    output_w,
    down,
    up_query,
    up_key,
    up_value,
    cache_key,
    cache_value,
    send1,
    recv1,
    send2,
    recv2,
    send3,
    recv3,
    stage_q,
    stage_kv,
    send4,
    recv4,
    send5,
    recv5,
    send6,
    recv6,
    local_sem,
    query_sem,
    ssem1,
    rsem1,
    ssem2,
    rsem2,
    ssem3,
    rsem3,
    ssem4,
    rsem4,
    ssem5,
    rsem5,
    ssem6,
    rsem6,
):
    me_b = lax.axis_index("batch")
    me_t = lax.axis_index("tensor")

    def fetch(src, dst, sem):
        copy = pltpu.make_async_copy(src, dst, sem)
        copy.start()
        return copy

    get_tokens = fetch(tokens_hbm, tokens, local_sem.at[0])
    get_down = fetch(down_hbm, down.at[:, pl.ds(0, 48), :], local_sem.at[1])
    get_up = [
        fetch(up_query_hbm, up_query, local_sem.at[2]),
        fetch(up_key_hbm, up_key, local_sem.at[3]),
        fetch(up_value_hbm, up_value, local_sem.at[4]),
    ]
    get_kv = [
        fetch(key_hbm, kv_w.at[pl.ds(0, 64), :], local_sem.at[5]),
        fetch(value_hbm, kv_w.at[pl.ds(64, 64), :], local_sem.at[6]),
    ]
    piece = DEPTH // QUERY_CHUNKS
    get_query = [
        fetch(
            query_hbm.at[pl.ds(i * piece, piece), :],
            query_w.at[pl.ds(i * piece, piece), :],
            query_sem.at[i],
        )
        for i in range(QUERY_CHUNKS)
    ]
    get_key = fetch(cache_key_hbm, cache_key, local_sem.at[7])
    get_value = fetch(cache_value_hbm, cache_value, local_sem.at[8])
    get_output = [
        fetch(
            output_hbm.at[pl.ds(i * 128, 128), :],
            output_w.at[pl.ds(i * 128, 128), :],
            local_sem.at[9 + i],
        )
        for i in range(4)
    ]

    barrier = pltpu.get_barrier_semaphore()

    def greet_b(i, carry):
        peer = lax.rem(me_b + i, GROUPS)
        pl.semaphore_signal(barrier, inc=1, device_id={"batch": peer}, device_id_type=MESH)
        return carry

    def greet_t(i, carry):
        peer = lax.rem(me_t + i, SPLIT)
        pl.semaphore_signal(barrier, inc=1, device_id={"tensor": peer}, device_id_type=MESH)
        return carry

    lax.fori_loop(1, GROUPS, greet_b, 0)
    lax.fori_loop(1, SPLIT, greet_t, 0)

    down[:, pl.ds(48, 80), :] = jnp.zeros((4, 80, COLS), BF16)

    row_i = iota((ROWS, ROWS), 0)
    col_i = iota((ROWS, ROWS), 1)
    diag = row_i == col_i
    index_c = jnp.broadcast_to(index_ref[...].astype(F32), (ROWS, ROWS))
    store_c = jnp.broadcast_to(store_ref[...].astype(F32), (ROWS, ROWS))
    index_r = jnp.sum(jnp.where(diag, index_c, 0.0), axis=1, keepdims=True)
    slot_r = jnp.sum(
        jnp.where(index_r == col_i.astype(F32), store_c, 0.0), axis=1, keepdims=True
    )
    slot_c = jnp.sum(jnp.where(diag, slot_r, 0.0), axis=0, keepdims=True)
    owner_r = jnp.floor(slot_r * 0.25)
    owner_c = jnp.floor(slot_c * 0.25)
    within_r = slot_r - 4.0 * owner_r
    place_c = jnp.sum(
        jnp.where((owner_r == owner_c) & (row_i < col_i), 1.0, 0.0), axis=0, keepdims=True
    )
    target_c = owner_c * CAP + place_c
    slots = GROUPS * CAP
    route = jnp.where(target_c == iota((slots, ROWS), 0).astype(F32), 1.0, 0.0).astype(BF16)
    hot = jnp.where(within_r == iota((ROWS, 128), 1).astype(F32), 1.0, 0.0).astype(BF16)

    get_tokens.wait()
    own = tokens[:, pl.ds(pl.multiple_of(me_t * COLS, COLS), COLS)]
    routed = dot(route, own).reshape(GROUPS, CAP, COLS)
    routed_hot = dot(route, hot).reshape(GROUPS, CAP, 128)
    send1[:, :, 0:256] = jnp.concatenate(
        [routed[:, :, 0:256], routed[:, :, 256:512]], axis=1
    ).astype(BF16)
    send1[:, :, 256:384] = jnp.concatenate(
        [routed_hot, jnp.zeros_like(routed_hot)], axis=1
    ).astype(BF16)

    pl.semaphore_wait(barrier, GROUPS - 1 + SPLIT - 1)

    def start_all(axis, me, count, source, target, ssem, rsem):
        def body(i, carry):
            peer = lax.rem(me + i, count)
            pltpu.make_async_remote_copy(
                src_ref=source(peer),
                dst_ref=target.at[me],
                send_sem=ssem.at[peer],
                recv_sem=rsem.at[me],
                device_id={axis: peer},
                device_id_type=MESH,
            ).start()
            return carry

        lax.fori_loop(1, count, body, 0)

    def wait_all(axis, me, count, source, target, ssem, rsem, which):
        def body(i, carry):
            peer = lax.rem(me + i, count)
            copy = pltpu.make_async_remote_copy(
                src_ref=source(peer),
                dst_ref=target.at[peer],
                send_sem=ssem.at[peer],
                recv_sem=rsem.at[peer],
                device_id={axis: peer},
                device_id_type=MESH,
            )
            if which == "recv":
                copy.wait_recv()
            else:
                copy.wait_send()
            return carry

        lax.fori_loop(1, count, body, 0)

    phase1 = ("batch", me_b, GROUPS, lambda p: send1.at[p], recv1, ssem1, rsem1)
    start_all(*phase1)
    recv1[me_b] = send1[me_b]

    for copy in get_kv:
        copy.wait()
    kv_base = dot_tb(tokens[...], kv_w[...])

    def query_part(total, chunks):
        for i in chunks:
            get_query[i].wait()
            total = total + dot(
                tokens[:, i * piece : (i + 1) * piece], query_w[i * piece : (i + 1) * piece, :]
            )
        return total

    q_base = jnp.zeros((ROWS, COLS), F32)

    wait_all(*phase1, "recv")
    got = recv1[...].astype(F32)
    rows_in = jnp.concatenate([got[:, 0:8, 0:256], got[:, 8:16, 0:256]], axis=2).reshape(
        slots, COLS
    )
    hot_in = got[:, 0:8, 256:384].reshape(slots, 128)
    get_down.wait()
    shrunk = jnp.zeros((slots, 128), F32)
    for a in range(4):
        shrunk = shrunk + dot_tb((rows_in * hot_in[:, a : a + 1]).astype(BF16), down[a])
    send2[...] = (shrunk[0:32] + pltpu.roll(shrunk[32:64], 64, 1)).astype(BF16)

    phase2 = ("tensor", me_t, SPLIT, lambda p: send2, recv2, ssem2, rsem2)
    start_all(*phase2)
    recv2[me_t] = send2[...]

    q_base = query_part(q_base, range(0, 4))

    wait_all(*phase2, "recv")
    summed = jnp.sum(recv2[...].astype(F32), axis=0)
    scaled = (ADAPTER_SCALE * summed).astype(BF16)
    lane_in = iota((128, 256), 0)
    lane_out = iota((128, 256), 1)
    wanted = (lane_out // 64) * 16 + lane_out % 16
    pick_lo = jnp.where((lane_in == wanted) & (lane_out < 192), 1.0, 0.0).astype(BF16)
    pick_hi = jnp.where((lane_in == wanted + 64) & (lane_out < 192), 1.0, 0.0).astype(BF16)
    spread_hot = jnp.where(lane_in == (lane_out % 64) // 16, 1.0, 0.0).astype(BF16)
    spread = jnp.concatenate([dot(scaled, pick_lo), dot(scaled, pick_hi)], axis=0)
    masked = (spread * dot(hot_in.astype(BF16), spread_hot)).astype(BF16)
    for copy in get_up:
        copy.wait()
    delta_q = dot(masked[:, 0:64], up_query[...].reshape(64, COLS))
    delta_k = dot(masked[:, 64:128], up_key[...].reshape(64, 64))
    delta_v = dot(masked[:, 128:192], up_value[...].reshape(64, 64))
    delta_kv = jnp.concatenate([delta_k, delta_v], axis=1)
    delta_q = delta_q.reshape(GROUPS, CAP, COLS)
    delta_kv = delta_kv.reshape(GROUPS, CAP, 128)
    send3[:, :, 0:256] = jnp.concatenate(
        [delta_q[:, :, 0:256], delta_q[:, :, 256:512]], axis=1
    ).astype(BF16)
    send3[:, :, 256:384] = jnp.concatenate(
        [delta_kv, jnp.zeros_like(delta_kv)], axis=1
    ).astype(BF16)

    phase3 = ("batch", me_b, GROUPS, lambda p: send3.at[p], recv3, ssem3, rsem3)
    start_all(*phase3)
    recv3[me_b] = send3[me_b]

    q_base = query_part(q_base, range(4, QUERY_CHUNKS))

    wait_all(*phase3, "recv")
    back = recv3[...].astype(F32)
    back = jnp.concatenate(
        [back[:, 0:8, 0:256], back[:, 8:16, 0:256], back[:, 0:8, 256:384]], axis=2
    ).reshape(slots, COLS + 128)
    delta = lax.dot_general(
        route, back.astype(BF16), (((0,), (0,)), ((), ())), preferred_element_type=F32
    )
    q_new = q_base + delta[:, 0:COLS]
    kv_new = kv_base + delta[:, COLS:]
    parity = lax.rem(me_t, 2)
    rolled = pltpu.roll(kv_new, 64, 1)
    half = iota((ROWS, 128), 1) // 64 == parity
    k_row = jnp.where(half, jnp.where(parity == 1, rolled, kv_new), 0.0)
    v_row = jnp.where(half, jnp.where(parity == 1, kv_new, rolled), 0.0)
    stage_kv[...] = jnp.zeros_like(stage_kv)
    for j in range(4):
        stage_q[pl.ds(j, ROWS, stride=4), :] = q_new[:, 128 * j : 128 * (j + 1)]
    stage_kv[pl.ds(0, ROWS, stride=4), :] = k_row
    stage_kv[pl.ds(1, ROWS, stride=4), :] = v_row
    send4[...] = jnp.concatenate(
        [stage_q[...].reshape(SPLIT, 8, 128), stage_kv[...].reshape(SPLIT, 8, 128)], axis=1
    ).astype(BF16)

    phase4 = ("tensor", me_t, SPLIT, lambda p: send4.at[p], recv4, ssem4, rsem4)
    start_all(*phase4)
    recv4[me_t] = send4[me_t]

    lane = iota((1, 128), 1)
    lane_row = (lane % 8) // 4
    length_lane = iota((1, ROWS), 1)
    lengths = length_ref[...].astype(F32)
    length0 = jnp.sum(jnp.where(length_lane == 2 * me_t, lengths, 0.0), axis=1, keepdims=True)
    length1 = jnp.sum(jnp.where(length_lane == 2 * me_t + 1, lengths, 0.0), axis=1, keepdims=True)
    limit = jnp.where(lane_row == 0, length0, length1)

    wait_all(*phase4, "recv")
    arrived = recv4[...].astype(F32)
    q_all = arrived[:, 0:8, :].reshape(128, 128)
    kv_all = jnp.sum(arrived[:, 8:16, :].reshape(8, 2, 8, 128), axis=1)
    tail = jnp.concatenate([kv_all[g] for g in range(8)], axis=1)
    head_row = iota((128, 128), 0) // 16
    blocks = jnp.concatenate(
        [jnp.where(head_row == g, q_all, 0.0).astype(BF16) for g in range(8)], axis=1
    )
    get_key.wait()
    scores = jnp.where(
        lane_row == 0, dot_tb(cache_key[0], blocks), dot_tb(cache_key[1], blocks)
    )
    self_scores = dot_tb(tail.astype(BF16), blocks)
    score_scale = 1.0 / math.sqrt(HEAD_WIDTH)
    valid = iota((SPAN, 128), 0).astype(F32) < limit
    scores = jnp.where(valid, scores * score_scale, MASKED_SCORE)
    self_valid = iota((8, 128), 0) == 4 * lane_row
    self_scores = jnp.where(self_valid, self_scores * score_scale, MASKED_SCORE)
    top = jnp.maximum(
        jnp.max(scores, axis=0, keepdims=True), jnp.max(self_scores, axis=0, keepdims=True)
    )
    weights = jnp.exp(scores - top)
    self_weight = jnp.exp(self_scores - top)
    full_total = jnp.sum(weights, axis=0, keepdims=True) + jnp.sum(
        self_weight, axis=0, keepdims=True
    )
    weights_t = jnp.transpose(weights).astype(BF16)
    extra_t = jnp.transpose(
        jnp.concatenate(
            [self_weight, jnp.broadcast_to(full_total, (8, 128)), jnp.zeros((112, 128), F32)],
            axis=0,
        )
    )
    self_t = extra_t[:, 0:8].astype(BF16)
    total_t = extra_t[:, 8:9]
    tail_v = pltpu.roll(tail, 7, 0).astype(BF16)
    get_value.wait()
    row_of = (iota((32, 128), 0) % 8) // 4
    attended = []
    for pair in range(4):
        part = weights_t[32 * pair : 32 * (pair + 1), :]
        cols = slice(256 * pair, 256 * (pair + 1))
        over = [dot(part, cache_value[r, :, cols]) for r in range(2)]
        last = dot(self_t[32 * pair : 32 * (pair + 1), :], tail_v[:, cols])
        both = [o + last for o in over]
        mine = [jnp.concatenate([o[0:16, 0:128], o[16:32, 128:256]], axis=0) for o in both]
        attended.append(jnp.where(row_of == 0, mine[0], mine[1]))
    send5[...] = (jnp.concatenate(attended, axis=0) / total_t).reshape(SPLIT, 8, 128)

    phase5 = ("tensor", me_t, SPLIT, lambda p: send5.at[p], recv5, ssem5, rsem5)
    start_all(*phase5)
    recv5[me_t] = send5[me_t]
    for copy in get_output:
        copy.wait()
    wait_all(*phase5, "recv")
    stage_q[...] = recv5[...].reshape(128, 128)
    heads = jnp.concatenate(
        [stage_q[pl.ds(j, ROWS, stride=4), :].astype(BF16) for j in range(4)], axis=1
    )

    def project(i, carry):
        peer = lax.rem(me_t + i, SPLIT)
        cols = pl.ds(pl.multiple_of(peer * COLS, COLS), COLS)
        send6[peer] = dot(heads, output_w[:, cols]).astype(BF16)
        pltpu.make_async_remote_copy(
            src_ref=send6.at[peer],
            dst_ref=recv6.at[me_t],
            send_sem=ssem6.at[peer],
            recv_sem=rsem6.at[me_t],
            device_id={"tensor": peer},
            device_id_type=MESH,
        ).start()
        return carry

    lax.fori_loop(1, SPLIT, project, 0)
    own_cols = pl.ds(pl.multiple_of(me_t * COLS, COLS), COLS)
    total = dot(heads, output_w[:, own_cols])

    phase6 = ("tensor", me_t, SPLIT, lambda p: send6.at[p], recv6, ssem6, rsem6)
    wait_all(*phase6, "recv")

    def add_up(i, total):
        return total + recv6[lax.rem(me_t + i, SPLIT)].astype(F32)

    total = lax.fori_loop(1, SPLIT, add_up, total)
    out_ref[...] = total.astype(BF16)

    for phase in (phase1, phase2, phase3, phase4, phase5, phase6):
        wait_all(*phase, "send")


def on_device(
    tokens,
    row_adapter_index,
    adapter_store_row,
    lengths,
    query_weight,
    key_weight,
    value_weight,
    output_weight,
    adapter_down_weight,
    adapter_up_query,
    adapter_up_key,
    adapter_up_value,
    cached_key_rows,
    cached_value_rows,
):
    small = pl.BlockSpec(memory_space=pltpu.VMEM)
    large = pl.BlockSpec(memory_space=pltpu.HBM)
    dma = pltpu.SemaphoreType.DMA
    return pl.pallas_call(
        kernel,
        out_shape=jax.ShapeDtypeStruct((ROWS, COLS), BF16),
        in_specs=[small] * 3 + [large] * 11,
        out_specs=small,
        scratch_shapes=[
            pltpu.VMEM((ROWS, DEPTH), BF16),
            pltpu.VMEM((DEPTH, COLS), BF16),
            pltpu.VMEM((128, DEPTH), BF16),
            pltpu.VMEM((COLS, DEPTH), BF16),
            pltpu.VMEM((4, 128, COLS), BF16),
            pltpu.VMEM((4, 16, COLS), BF16),
            pltpu.VMEM((4, 16, 64), BF16),
            pltpu.VMEM((4, 16, 64), BF16),
            pltpu.VMEM((2, SPAN, 1024), BF16),
            pltpu.VMEM((2, SPAN, 1024), BF16),
            pltpu.VMEM((GROUPS, 16, 384), BF16),
            pltpu.VMEM((GROUPS, 16, 384), BF16),
            pltpu.VMEM((32, 128), BF16),
            pltpu.VMEM((SPLIT, 32, 128), BF16),
            pltpu.VMEM((GROUPS, 16, 384), BF16),
            pltpu.VMEM((GROUPS, 16, 384), BF16),
            pltpu.VMEM((128, 128), F32),
            pltpu.VMEM((128, 128), F32),
            pltpu.VMEM((SPLIT, 16, 128), BF16),
            pltpu.VMEM((SPLIT, 16, 128), BF16),
            pltpu.VMEM((SPLIT, 8, 128), F32),
            pltpu.VMEM((SPLIT, 8, 128), F32),
            pltpu.VMEM((SPLIT, ROWS, COLS), BF16),
            pltpu.VMEM((SPLIT, ROWS, COLS), BF16),
            dma((13,)),
            dma((QUERY_CHUNKS,)),
            dma((GROUPS,)),
            dma((GROUPS,)),
            dma((SPLIT,)),
            dma((SPLIT,)),
            dma((GROUPS,)),
            dma((GROUPS,)),
            dma((SPLIT,)),
            dma((SPLIT,)),
            dma((SPLIT,)),
            dma((SPLIT,)),
            dma((SPLIT,)),
            dma((SPLIT,)),
        ],
        compiler_params=pltpu.CompilerParams(
            collective_id=0, has_side_effects=True, vmem_limit_bytes=56 * 1024 * 1024
        ),
    )(
        row_adapter_index.reshape(1, ROWS),
        adapter_store_row.reshape(1, 32),
        lengths.reshape(1, ROWS),
        tokens,
        query_weight,
        key_weight.T,
        value_weight.T,
        output_weight,
        adapter_down_weight,
        adapter_up_query,
        adapter_up_key,
        adapter_up_value,
        cached_key_rows,
        cached_value_rows,
    )


def solution(mesh):
    placed = (
        P("batch", None),
        P("batch"),
        P(),
        P("batch"),
        P(None, "tensor"),
        P(None, "tensor"),
        P(None, "tensor"),
        P("tensor", None),
        P("batch", None, "tensor"),
        P("batch", None, "tensor"),
        P("batch", None, "tensor"),
        P("batch", None, "tensor"),
        P(("batch", "tensor"), None, None),
        P(("batch", "tensor"), None, None),
    )
    return jax.shard_map(
        on_device, mesh=mesh, in_specs=placed, out_specs=P("batch", "tensor"), check_vma=False
    )
```

time: 263 us -> 48.7 us (0.19)
  the two profiles are of different devices: /device:TPU:0 before, /device:TPU:1 now
where the time goes in v1:
time: 48.7 us; the launch traced here: 48.5 us
  Pallas kernels  47.1 us (97%)
  local copies, waits for them, and re-layouts  1.38 us (3%)
    pallas_call x1, Pallas kernels, on_device(): pl.pallas_call(kernel, out_shape=jax.ShapeDtypeStruct((ROWS, COLS), BF16)...  47.1 us
    unnamed x1, local copies, waits for them, and re-layouts  1.38 us

profile of v1, /device:TPU:1, one launch (start us, length us, event | category | flops | bytes accessed | tf_op | source)
XLA Modules:
  0.0 48.5 jit_solution(8040522897521726369)
XLA Ops:
  0.0 47.1 %shard_map.136 = bf16[32,512]{1,0:T(8,128)(2,1)} custom-call(s32[1,32]{1,0:T(1,128)} %bitcast.7, s32[1,32]{1,0:T(1,128)} %bitcast.8, s32[1,32]{1,0:T(1,128)} %bitcast.9, bf16[32,8192]{1,0:T(8,128)(2,1)} %tokens_hbm.1, bf16[8192,512]{1,0:T(8,128)(2,1)} %query_hbm.1, bf16[64,8192]{1,0:T(8,128)(2,1)} %bitcast.5, bf16[64,8192]{1,0:T(8,128)(2,1)} %bitcast.6, ...), custom_call_target="tpu_custom_call" | custom-call | tf_op jit(solution)/shard_map/pallas_call | solution.py:435
  47.1 1.4 %copy.16 = bf16[32,512]{1,0:T(8,128)(2,1)} copy(bf16[32,512]{1,0:T(8,128)(2,1)} %shard_map.136) | data formatting | bytes 65536

commit v2 on v1

v2 whole, which is shorter than its diff:
```python
import math

import jax
import jax.numpy as jnp
from jax import lax
from jax.experimental import pallas as pl
from jax.experimental.pallas import tpu as pltpu
from jax.sharding import PartitionSpec as P

HEAD_WIDTH = 128
ADAPTER_SCALE = 0.5
MASKED_SCORE = -1e30
MESH = pl.DeviceIdType.MESH
F32 = jnp.float32
BF16 = jnp.bfloat16

GROUPS = 8
SPLIT = 16
CAP = 8
ROWS = 32
QUERY_CHUNKS = 8
DEPTH = 8192
COLS = 512
SPAN = 512
TRANS_B = (((1,), (1,)), ((), ()))


def iota(shape, dim):
    return lax.broadcasted_iota(jnp.int32, shape, dim)


def dot(a, b):
    return jnp.dot(a, b, preferred_element_type=F32)


def dot_tb(a, b):
    return lax.dot_general(a, b, TRANS_B, preferred_element_type=F32)


def far_first(count):
    steps = [(dy, dz) for dy in range(4) for dz in range(4) if dy or dz]
    return sorted(steps, key=lambda s: -(min(s[0], 4 - s[0]) + min(s[1], 4 - s[1])))


TENSOR_STEPS = far_first(SPLIT)
BATCH_STEPS = [(2, 1), (2, 0), (1, 1), (3, 1), (1, 0), (3, 0), (0, 1)]


def kernel(
    index_hbm,
    store_hbm,
    length_hbm,
    tokens_hbm,
    query_hbm,
    key_hbm,
    value_hbm,
    output_hbm,
    down_hbm,
    up_query_hbm,
    up_key_hbm,
    up_value_hbm,
    cache_key_hbm,
    cache_value_hbm,
    out_ref,
    index_ref,
    store_ref,
    length_ref,
    own_tokens,
    tokens,
    query_w,
    kv_w,
    output_w,
    down,
    up_query,
    up_key,
    up_value,
    cache_key,
    cache_value,
    send1,
    recv1,
    send2,
    recv2,
    send3,
    recv3,
    stage_q,
    stage_kv,
    send4,
    recv4,
    send5,
    recv5,
    send6,
    recv6,
    local_sem,
    query_sem,
    send_sem,
    rsem1,
    rsem2,
    rsem3,
    rsem4,
    rsem5,
    rsem6,
):
    me_b = lax.axis_index("batch")
    me_t = lax.axis_index("tensor")
    me_x, me_c = me_b // 2, lax.rem(me_b, 2)
    me_y, me_z = me_t // 4, lax.rem(me_t, 4)

    def batch_peer(step):
        core = 1 - me_c if step[1] else me_c
        return lax.rem(me_x + step[0], 4) * 2 + core

    def tensor_peer(step):
        return lax.rem(me_y + step[0], 4) * 4 + lax.rem(me_z + step[1], 4)

    batch_peers = [batch_peer(step) for step in BATCH_STEPS]
    tensor_peers = [tensor_peer(step) for step in TENSOR_STEPS]

    barrier = pltpu.get_barrier_semaphore()
    for peer in tensor_peers:
        pl.semaphore_signal(barrier, inc=1, device_id={"tensor": peer}, device_id_type=MESH)
    for peer in batch_peers:
        pl.semaphore_signal(barrier, inc=1, device_id={"batch": peer}, device_id_type=MESH)

    pending = []

    def fetch(src, dst, sem):
        copy = pltpu.make_async_copy(src, dst, sem)
        copy.start()
        pending.append(copy)
        return copy

    def need(*copies):
        for copy in copies:
            if any(copy is other for other in pending):
                pending[:] = [other for other in pending if other is not copy]
                copy.wait()

    own_cols = pl.ds(pl.multiple_of(me_t * COLS, COLS), COLS)
    get_index = fetch(index_hbm, index_ref, local_sem.at[0])
    get_store = fetch(store_hbm, store_ref, local_sem.at[1])
    get_own = fetch(tokens_hbm.at[:, own_cols], own_tokens, local_sem.at[2])
    get_down = [
        fetch(down_hbm.at[a], down.at[pl.ds(64 * a, 48), :], local_sem.at[3 + a]) for a in range(4)
    ]
    get_up = [
        fetch(up_query_hbm, up_query, local_sem.at[7]),
        fetch(up_key_hbm, up_key, local_sem.at[8]),
        fetch(up_value_hbm, up_value, local_sem.at[9]),
    ]
    get_length = fetch(length_hbm, length_ref, local_sem.at[10])
    get_tokens = fetch(tokens_hbm, tokens, local_sem.at[11])
    get_kv = [
        fetch(key_hbm, kv_w.at[pl.ds(0, 64), :], local_sem.at[12]),
        fetch(value_hbm, kv_w.at[pl.ds(64, 64), :], local_sem.at[13]),
    ]
    piece = DEPTH // QUERY_CHUNKS
    get_query = [
        fetch(
            query_hbm.at[pl.ds(i * piece, piece), :],
            query_w.at[pl.ds(i * piece, piece), :],
            query_sem.at[i],
        )
        for i in range(QUERY_CHUNKS)
    ]
    get_key = fetch(cache_key_hbm, cache_key, local_sem.at[14])
    get_value = fetch(cache_value_hbm, cache_value, local_sem.at[15])
    get_output = [
        fetch(
            output_hbm.at[pl.ds(i * 128, 128), :],
            output_w.at[pl.ds(i * 128, 128), :],
            local_sem.at[16 + i],
        )
        for i in range(4)
    ]

    row_i = iota((ROWS, ROWS), 0)
    col_i = iota((ROWS, ROWS), 1)
    diag = row_i == col_i
    need(get_index, get_store)
    index_c = jnp.broadcast_to(index_ref[...].astype(F32), (ROWS, ROWS))
    store_c = jnp.broadcast_to(store_ref[...].astype(F32), (ROWS, ROWS))
    index_r = jnp.sum(jnp.where(diag, index_c, 0.0), axis=1, keepdims=True)
    slot_r = jnp.sum(
        jnp.where(index_r == col_i.astype(F32), store_c, 0.0), axis=1, keepdims=True
    )
    slot_c = jnp.sum(jnp.where(diag, slot_r, 0.0), axis=0, keepdims=True)
    owner_r = jnp.floor(slot_r * 0.25)
    owner_c = jnp.floor(slot_c * 0.25)
    within_r = slot_r - 4.0 * owner_r
    same = owner_r == owner_c
    place_c = jnp.sum(jnp.where(same & (row_i < col_i), 1.0, 0.0), axis=0, keepdims=True)
    target_c = owner_c * 16.0 + place_c
    slot_i = iota((128, ROWS), 0)
    route = jnp.where(
        target_c == ((slot_i // 16) * 16 + slot_i % 8).astype(F32), 1.0, 0.0
    ).astype(BF16)
    hot = jnp.where(within_r == iota((ROWS, 128), 1).astype(F32), 1.0, 0.0).astype(BF16)
    lower = (iota((128, 256), 0) % 16) < 8

    need(get_own)
    routed = dot(route, own_tokens[...])
    routed_hot = dot(route, hot)
    send1[:, :, 0:256] = (
        jnp.where(lower, routed[:, 0:256], routed[:, 256:512]).astype(BF16).reshape(GROUPS, 16, 256)
    )
    send1[:, :, 256:384] = routed_hot.astype(BF16).reshape(GROUPS, 16, 128)

    pl.semaphore_wait(barrier, GROUPS - 1 + SPLIT - 1)

    def remote(axis, peer, source, target, phase, rsem):
        return pltpu.make_async_remote_copy(
            src_ref=source,
            dst_ref=target,
            send_sem=send_sem.at[phase],
            recv_sem=rsem,
            device_id={axis: peer},
            device_id_type=MESH,
        )

    def start_batch(phase, send, recv, rsem):
        for peer in batch_peers:
            remote("batch", peer, send.at[peer], recv.at[me_b], phase, rsem.at[me_b]).start()

    def wait_batch(phase, send, recv, rsem):
        for peer in batch_peers[::-1]:
            remote("batch", peer, send.at[peer], recv.at[peer], phase, rsem.at[peer]).wait_recv()

    def sent(phase, like):
        pltpu.make_async_copy(like, like, send_sem.at[phase]).wait()

    start_batch(0, send1, recv1, rsem1)
    recv1[me_b] = send1[me_b]

    for a in range(4):
        down[pl.ds(64 * a + 48, 16), :] = jnp.zeros((16, COLS), BF16)
    place_r = jnp.sum(jnp.where(same & (col_i < row_i), 1.0, 0.0), axis=1, keepdims=True)
    target_r = owner_r * 16.0 + place_r
    slot_j = iota((ROWS, 128), 1).astype(F32)
    unroute = jnp.concatenate(
        [
            jnp.where(target_r == slot_j, 1.0, 0.0),
            jnp.where(target_r + 8.0 == slot_j, 1.0, 0.0),
        ],
        axis=0,
    ).astype(BF16)
    lane_in = iota((128, 256), 0)
    lane_out = iota((128, 256), 1)
    group_hot = jnp.where(lane_in == lane_out // 64, 1.0, 0.0).astype(BF16)
    turn = jnp.where(lane_out < 64, 16, jnp.where(lane_out < 128, 32, 0))
    wanted = jnp.where(lane_out < 192, turn + lane_out % 16, -256)
    pick = jnp.concatenate(
        [jnp.where(lane_in == wanted, 1.0, 0.0), jnp.where(lane_in == wanted + 64, 1.0, 0.0)],
        axis=1,
    ).astype(BF16)
    spread_hot = jnp.where(lane_in == (lane_out % 64) // 16, 1.0, 0.0).astype(BF16)

    need(get_tokens, *get_kv)
    kv_base = dot_tb(tokens[...], kv_w[...])

    def query_part(total, chunks):
        for i in chunks:
            need(get_query[i])
            total = total + dot(
                tokens[:, i * piece : (i + 1) * piece], query_w[i * piece : (i + 1) * piece, :]
            )
        return total

    q_base = query_part(jnp.zeros((ROWS, COLS), F32), range(0, 3))
    need(*get_down)

    wait_batch(0, send1, recv1, rsem1)
    rows_in = recv1[:, :, 0:256].reshape(128, 256)
    hot_in = recv1[:, :, 256:384].reshape(128, 128)
    empty = jnp.zeros_like(rows_in)
    rows_in = jnp.concatenate(
        [jnp.where(lower, rows_in, empty), jnp.where(lower, empty, rows_in)], axis=1
    )
    shrunk = dot_tb(rows_in, down[...]) * dot(hot_in, group_hot)
    shrunk = shrunk[:, 0:128] + shrunk[:, 128:256]
    shrunk = jnp.sum(shrunk.reshape(GROUPS, 2, CAP, 128), axis=1).reshape(64, 128)
    shrunk = shrunk + pltpu.roll(shrunk, 64, 1)
    send2[...] = jnp.where(iota((32, 128), 1) < 64, shrunk[0:32], shrunk[32:64]).astype(BF16)

    for peer in tensor_peers:
        remote("tensor", peer, send2, recv2.at[me_t], 1, rsem2.at[me_t]).start()

    hot_rows = dot(hot_in, spread_hot).reshape(GROUPS, 2, CAP, 256)[:, 0].reshape(64, 256)
    need(*get_up)
    up_k = up_key[...].reshape(64, 64)
    up_v = up_value[...].reshape(64, 64)
    blank = jnp.zeros_like(up_k)
    up_kv = jnp.concatenate(
        [jnp.concatenate([up_k, blank], axis=1), jnp.concatenate([blank, up_v], axis=1)], axis=0
    )
    q_base = query_part(q_base, range(3, QUERY_CHUNKS))

    summed = send2[...].astype(F32)
    for peer in tensor_peers[::-1]:
        remote("tensor", peer, send2, recv2.at[peer], 1, rsem2.at[peer]).wait_recv()
        summed = summed + recv2[peer].astype(F32)
    scaled = (ADAPTER_SCALE * summed).astype(BF16)
    spread = dot(scaled, pick)
    spread = jnp.concatenate([spread[:, 0:256], spread[:, 256:512]], axis=0)
    masked = (spread * hot_rows).astype(BF16)
    delta_kv = dot(masked[:, 0:128], up_kv).reshape(GROUPS, CAP, 128)
    delta_q = dot(masked[:, 128:192], up_query[...].reshape(64, COLS)).reshape(GROUPS, CAP, COLS)
    send3[:, :, 0:256] = jnp.concatenate(
        [delta_q[:, :, 0:256], delta_q[:, :, 256:512]], axis=1
    ).astype(BF16)
    send3[:, :, 256:384] = jnp.concatenate([delta_kv, delta_kv], axis=1).astype(BF16)

    start_batch(2, send3, recv3, rsem3)
    recv3[me_b] = send3[me_b]

    parity = lax.rem(me_t, 2)
    half = iota((ROWS, 128), 1) // 64 == parity
    stage_kv[...] = jnp.zeros_like(stage_kv)
    need(get_length)
    lane = iota((1, 128), 1)
    lane_row = (lane % 8) // 4
    length_lane = iota((1, ROWS), 1)
    lengths = length_ref[...].astype(F32)
    length0 = jnp.sum(jnp.where(length_lane == 2 * me_t, lengths, 0.0), axis=1, keepdims=True)
    length1 = jnp.sum(jnp.where(length_lane == 2 * me_t + 1, lengths, 0.0), axis=1, keepdims=True)
    limit = jnp.where(lane_row == 0, length0, length1)

    wait_batch(2, send3, recv3, rsem3)
    delta = dot(unroute, recv3[...].reshape(128, 384))
    kv_new = kv_base + delta[0:32, 256:384]
    rolled = pltpu.roll(kv_new, 64, 1)
    k_row = jnp.where(half, jnp.where(parity == 1, rolled, kv_new), 0.0)
    v_row = jnp.where(half, jnp.where(parity == 1, kv_new, rolled), 0.0)
    for j in range(4):
        part = delta[32 * (j // 2) : 32 * (j // 2) + 32, 128 * (j % 2) : 128 * (j % 2) + 128]
        stage_q[pl.ds(j, ROWS, stride=4), :] = q_base[:, 128 * j : 128 * (j + 1)] + part
    stage_kv[pl.ds(0, ROWS, stride=4), :] = k_row
    stage_kv[pl.ds(1, ROWS, stride=4), :] = v_row
    send4[...] = jnp.concatenate(
        [stage_q[...].reshape(SPLIT, 8, 128), stage_kv[...].reshape(SPLIT, 8, 128)], axis=1
    ).astype(BF16)

    for peer in tensor_peers:
        remote("tensor", peer, send4.at[peer], recv4.at[me_t], 3, rsem4.at[me_t]).start()
    recv4[me_t] = send4[me_t]
    need(get_key, get_value, *get_output)
    score_scale = 1.0 / math.sqrt(HEAD_WIDTH)
    valid = iota((SPAN, 128), 0).astype(F32) < limit
    self_valid = iota((8, 128), 0) == 4 * lane_row
    head_row = iota((128, 128), 0) // 16
    row_of = (iota((32, 128), 0) % 8) // 4

    for peer in tensor_peers[::-1]:
        remote("tensor", peer, send4.at[peer], recv4.at[peer], 3, rsem4.at[peer]).wait_recv()
    arrived = recv4[...].astype(F32)
    q_all = arrived[:, 0:8, :].reshape(128, 128)
    kv_all = jnp.sum(arrived[:, 8:16, :].reshape(8, 2, 8, 128), axis=1)
    tail = jnp.concatenate([kv_all[g] for g in range(8)], axis=1)
    blocks = jnp.concatenate(
        [jnp.where(head_row == g, q_all, 0.0).astype(BF16) for g in range(8)], axis=1
    )
    scores = jnp.where(
        lane_row == 0, dot_tb(cache_key[0], blocks), dot_tb(cache_key[1], blocks)
    )
    self_scores = dot_tb(tail.astype(BF16), blocks)
    scores = jnp.where(valid, scores * score_scale, MASKED_SCORE)
    self_scores = jnp.where(self_valid, self_scores * score_scale, MASKED_SCORE)
    top = jnp.maximum(
        jnp.max(scores, axis=0, keepdims=True), jnp.max(self_scores, axis=0, keepdims=True)
    )
    weights = jnp.exp(scores - top)
    self_weight = jnp.exp(self_scores - top)
    full_total = jnp.sum(weights, axis=0, keepdims=True) + jnp.sum(
        self_weight, axis=0, keepdims=True
    )
    weights_t = jnp.transpose(weights).astype(BF16)
    extra_t = jnp.transpose(
        jnp.concatenate(
            [self_weight, jnp.broadcast_to(full_total, (8, 128)), jnp.zeros((112, 128), F32)],
            axis=0,
        )
    )
    self_t = extra_t[:, 0:8].astype(BF16)
    total_t = extra_t[:, 8:9]
    tail_v = pltpu.roll(tail, 7, 0).astype(BF16)
    attended = []
    for pair in range(4):
        part = weights_t[32 * pair : 32 * (pair + 1), :]
        cols = slice(256 * pair, 256 * (pair + 1))
        over = [dot(part, cache_value[r, :, cols]) for r in range(2)]
        last = dot(self_t[32 * pair : 32 * (pair + 1), :], tail_v[:, cols])
        both = [o + last for o in over]
        mine = [jnp.concatenate([o[0:16, 0:128], o[16:32, 128:256]], axis=0) for o in both]
        attended.append(jnp.where(row_of == 0, mine[0], mine[1]))
    send5[...] = jnp.concatenate(attended, axis=0) / total_t

    def eight(t):
        return pl.ds(pl.multiple_of(8 * t, 8), 8)

    for peer in tensor_peers:
        remote(
            "tensor", peer, send5.at[eight(peer)], recv5.at[eight(me_t)], 4, rsem5.at[me_t]
        ).start()
    recv5[eight(me_t), :] = send5[eight(me_t), :]
    sent(0, send1.at[pl.ds(0, GROUPS - 1)])
    sent(1, recv2.at[pl.ds(0, SPLIT - 1)])
    sent(2, send3.at[pl.ds(0, GROUPS - 1)])
    sent(3, send4.at[pl.ds(0, SPLIT - 1)])
    for peer in tensor_peers[::-1]:
        remote(
            "tensor", peer, send5.at[eight(peer)], recv5.at[eight(peer)], 4, rsem5.at[peer]
        ).wait_recv()
    heads = jnp.concatenate(
        [recv5[pl.ds(j, ROWS, stride=4), :].astype(BF16) for j in range(4)], axis=1
    )

    for peer in tensor_peers:
        cols = pl.ds(pl.multiple_of(peer * COLS, COLS), COLS)
        send6[peer] = dot(heads, output_w[:, cols]).astype(BF16)
        remote("tensor", peer, send6.at[peer], recv6.at[me_t], 5, rsem6.at[me_t]).start()
    total = dot(heads, output_w[:, own_cols])
    for dy, dz in TENSOR_STEPS:
        peer = tensor_peer((4 - dy, 4 - dz))
        remote("tensor", peer, send6.at[peer], recv6.at[peer], 5, rsem6.at[peer]).wait_recv()
        total = total + recv6[peer].astype(F32)
    out_ref[...] = total.astype(BF16)
    sent(4, send5.at[pl.ds(0, 8 * (SPLIT - 1))])
    sent(5, send6.at[pl.ds(0, SPLIT - 1)])


def on_device(
    tokens,
    row_adapter_index,
    adapter_store_row,
    lengths,
    query_weight,
    key_weight,
    value_weight,
    output_weight,
    adapter_down_weight,
    adapter_up_query,
    adapter_up_key,
    adapter_up_value,
    cached_key_rows,
    cached_value_rows,
):
    large = pl.BlockSpec(memory_space=pltpu.HBM)
    dma = pltpu.SemaphoreType.DMA
    return pl.pallas_call(
        kernel,
        out_shape=jax.ShapeDtypeStruct((ROWS, COLS), BF16),
        in_specs=[large] * 14,
        out_specs=pl.BlockSpec(memory_space=pltpu.VMEM),
        scratch_shapes=[
            pltpu.VMEM((1, ROWS), jnp.int32),
            pltpu.VMEM((1, 32), jnp.int32),
            pltpu.VMEM((1, ROWS), jnp.int32),
            pltpu.VMEM((ROWS, COLS), BF16),
            pltpu.VMEM((ROWS, DEPTH), BF16),
            pltpu.VMEM((DEPTH, COLS), BF16),
            pltpu.VMEM((128, DEPTH), BF16),
            pltpu.VMEM((COLS, DEPTH), BF16),
            pltpu.VMEM((256, COLS), BF16),
            pltpu.VMEM((4, 16, COLS), BF16),
            pltpu.VMEM((4, 16, 64), BF16),
            pltpu.VMEM((4, 16, 64), BF16),
            pltpu.VMEM((2, SPAN, 1024), BF16),
            pltpu.VMEM((2, SPAN, 1024), BF16),
            pltpu.VMEM((GROUPS, 16, 384), BF16),
            pltpu.VMEM((GROUPS, 16, 384), BF16),
            pltpu.VMEM((32, 128), BF16),
            pltpu.VMEM((SPLIT, 32, 128), BF16),
            pltpu.VMEM((GROUPS, 16, 384), BF16),
            pltpu.VMEM((GROUPS, 16, 384), BF16),
            pltpu.VMEM((128, 128), F32),
            pltpu.VMEM((128, 128), F32),
            pltpu.VMEM((SPLIT, 16, 128), BF16),
            pltpu.VMEM((SPLIT, 16, 128), BF16),
            pltpu.VMEM((128, 128), F32),
            pltpu.VMEM((128, 128), F32),
            pltpu.VMEM((SPLIT, ROWS, COLS), BF16),
            pltpu.VMEM((SPLIT, ROWS, COLS), BF16),
            dma((20,)),
            dma((QUERY_CHUNKS,)),
            dma((6,)),
            dma((GROUPS,)),
            dma((SPLIT,)),
            dma((GROUPS,)),
            dma((SPLIT,)),
            dma((SPLIT,)),
            dma((SPLIT,)),
        ],
        compiler_params=pltpu.CompilerParams(
            collective_id=0, has_side_effects=True, vmem_limit_bytes=56 * 1024 * 1024
        ),
    )(
        row_adapter_index.reshape(1, ROWS),
        adapter_store_row.reshape(1, 32),
        lengths.reshape(1, ROWS),
        tokens,
        query_weight,
        key_weight.T,
        value_weight.T,
        output_weight,
        adapter_down_weight,
        adapter_up_query,
        adapter_up_key,
        adapter_up_value,
        cached_key_rows,
        cached_value_rows,
    )


def solution(mesh):
    placed = (
        P("batch", None),
        P("batch"),
        P(),
        P("batch"),
        P(None, "tensor"),
        P(None, "tensor"),
        P(None, "tensor"),
        P("tensor", None),
        P("batch", None, "tensor"),
        P("batch", None, "tensor"),
        P("batch", None, "tensor"),
        P("batch", None, "tensor"),
        P(("batch", "tensor"), None, None),
        P(("batch", "tensor"), None, None),
    )
    return jax.shard_map(
        on_device, mesh=mesh, in_specs=placed, out_specs=P("batch", "tensor"), check_vma=False
    )
```

time: 48.7 us -> 43 us (0.88)
  the two profiles are of different devices: /device:TPU:1 before, /device:TPU:0 now
where the time goes in v2:
time: 43 us; the launch traced here: 42.8 us
  Pallas kernels  41.4 us (96%)
  local copies, waits for them, and re-layouts  1.38 us (3%)
    pallas_call x1, Pallas kernels, on_device(): pl.pallas_call(kernel, out_shape=jax.ShapeDtypeStruct((ROWS, COLS), BF16)...  41.4 us
    unnamed x1, local copies, waits for them, and re-layouts  1.38 us

profile of v2, /device:TPU:0, one launch (start us, length us, event | category | flops | bytes accessed | tf_op | source)
XLA Modules:
  0.0 42.8 jit_solution(10626787683271531990)
XLA Ops:
  0.0 41.4 %shard_map.136 = bf16[32,512]{1,0:T(8,128)(2,1)} custom-call(s32[1,32]{1,0:T(1,128)} %bitcast.7, s32[1,32]{1,0:T(1,128)} %bitcast.8, s32[1,32]{1,0:T(1,128)} %bitcast.9, bf16[32,8192]{1,0:T(8,128)(2,1)} %tokens_hbm.1, bf16[8192,512]{1,0:T(8,128)(2,1)} %query_hbm.1, bf16[64,8192]{1,0:T(8,128)(2,1)} %bitcast.5, bf16[64,8192]{1,0:T(8,128)(2,1)} %bitcast.6, ...), custom_call_target="tpu_custom_call" | custom-call | tf_op jit(solution)/shard_map/pallas_call | solution.py:448
  41.4 1.4 %copy.16 = bf16[32,512]{1,0:T(8,128)(2,1)} copy(bf16[32,512]{1,0:T(8,128)(2,1)} %shard_map.136) | data formatting | bytes 65536

commit v3 on v2

--- a/solution.py
+++ b/solution.py
@@ -43,6 +43,7 @@
 
 
 TENSOR_STEPS = far_first(SPLIT)
+PLANE_STEPS = (0, 1, 3, 2)
 BATCH_STEPS = [(2, 1), (2, 0), (1, 1), (3, 1), (1, 0), (3, 0), (0, 1)]
 
 
@@ -316,13 +317,10 @@
     half = iota((ROWS, 128), 1) // 64 == parity
     stage_kv[...] = jnp.zeros_like(stage_kv)
     need(get_length)
-    lane = iota((1, 128), 1)
-    lane_row = (lane % 8) // 4
     length_lane = iota((1, ROWS), 1)
     lengths = length_ref[...].astype(F32)
     length0 = jnp.sum(jnp.where(length_lane == 2 * me_t, lengths, 0.0), axis=1, keepdims=True)
     length1 = jnp.sum(jnp.where(length_lane == 2 * me_t + 1, lengths, 0.0), axis=1, keepdims=True)
-    limit = jnp.where(lane_row == 0, length0, length1)
 
     wait_batch(2, send3, recv3, rsem3)
     delta = dot(unroute, recv3[...].reshape(128, 384))
@@ -344,62 +342,76 @@
     recv4[me_t] = send4[me_t]
     need(get_key, get_value, *get_output)
     score_scale = 1.0 / math.sqrt(HEAD_WIDTH)
-    valid = iota((SPAN, 128), 0).astype(F32) < limit
-    self_valid = iota((8, 128), 0) == 4 * lane_row
-    head_row = iota((128, 128), 0) // 16
-    row_of = (iota((32, 128), 0) % 8) // 4
-
-    for peer in tensor_peers[::-1]:
-        remote("tensor", peer, send4.at[peer], recv4.at[peer], 3, rsem4.at[peer]).wait_recv()
-    arrived = recv4[...].astype(F32)
-    q_all = arrived[:, 0:8, :].reshape(128, 128)
-    kv_all = jnp.sum(arrived[:, 8:16, :].reshape(8, 2, 8, 128), axis=1)
-    tail = jnp.concatenate([kv_all[g] for g in range(8)], axis=1)
-    blocks = jnp.concatenate(
-        [jnp.where(head_row == g, q_all, 0.0).astype(BF16) for g in range(8)], axis=1
-    )
-    scores = jnp.where(
-        lane_row == 0, dot_tb(cache_key[0], blocks), dot_tb(cache_key[1], blocks)
-    )
-    self_scores = dot_tb(tail.astype(BF16), blocks)
-    scores = jnp.where(valid, scores * score_scale, MASKED_SCORE)
-    self_scores = jnp.where(self_valid, self_scores * score_scale, MASKED_SCORE)
-    top = jnp.maximum(
-        jnp.max(scores, axis=0, keepdims=True), jnp.max(self_scores, axis=0, keepdims=True)
-    )
-    weights = jnp.exp(scores - top)
-    self_weight = jnp.exp(self_scores - top)
-    full_total = jnp.sum(weights, axis=0, keepdims=True) + jnp.sum(
-        self_weight, axis=0, keepdims=True
-    )
-    weights_t = jnp.transpose(weights).astype(BF16)
-    extra_t = jnp.transpose(
-        jnp.concatenate(
-            [self_weight, jnp.broadcast_to(full_total, (8, 128)), jnp.zeros((112, 128), F32)],
-            axis=0,
-        )
-    )
-    self_t = extra_t[:, 0:8].astype(BF16)
-    total_t = extra_t[:, 8:9]
-    tail_v = pltpu.roll(tail, 7, 0).astype(BF16)
-    attended = []
-    for pair in range(4):
-        part = weights_t[32 * pair : 32 * (pair + 1), :]
-        cols = slice(256 * pair, 256 * (pair + 1))
-        over = [dot(part, cache_value[r, :, cols]) for r in range(2)]
-        last = dot(self_t[32 * pair : 32 * (pair + 1), :], tail_v[:, cols])
-        both = [o + last for o in over]
-        mine = [jnp.concatenate([o[0:16, 0:128], o[16:32, 128:256]], axis=0) for o in both]
-        attended.append(jnp.where(row_of == 0, mine[0], mine[1]))
-    send5[...] = jnp.concatenate(attended, axis=0) / total_t
+    row_of = (iota((32, 1), 0) % 8) // 4
+    key_of = iota((32, 1), 0) // 16
+    valid = iota((32, SPAN), 1).astype(F32) < jnp.where(row_of == 0, length0, length1)
+    self_valid = iota((32, 8), 1) == 4 * row_of
 
     def eight(t):
         return pl.ds(pl.multiple_of(8 * t, 8), 8)
 
-    for peer in tensor_peers:
-        remote(
-            "tensor", peer, send5.at[eight(peer)], recv5.at[eight(me_t)], 4, rsem5.at[me_t]
-        ).start()
+    def score(plane):
+        cols = pl.ds(pl.multiple_of(256 * plane, 256), 256)
+        arrived = recv4[pl.ds(4 * plane, 4)].astype(F32)
+        q = arrived[:, 0:8, :].reshape(32, 128)
+        kv = jnp.sum(arrived[:, 8:16, :].reshape(2, 2, 8, 128), axis=1)
+        tail = jnp.concatenate([kv[0], kv[1]], axis=1)
+        blocks = jnp.concatenate(
+            [jnp.where(key_of == 0, q, 0.0), jnp.where(key_of == 1, q, 0.0)], axis=1
+        ).astype(BF16)
+        scores = jnp.where(
+            row_of == 0,
+            dot_tb(blocks, cache_key[0, :, cols]),
+            dot_tb(blocks, cache_key[1, :, cols]),
+        )
+        self_scores = dot_tb(blocks, tail.astype(BF16))
+        scores = jnp.where(valid, scores * score_scale, MASKED_SCORE)
+        self_scores = jnp.where(self_valid, self_scores * score_scale, MASKED_SCORE)
+        return plane, scores, self_scores, pltpu.roll(tail, 7, 0).astype(BF16)
+
+    def attend(plane, scores, self_scores, tail_v):
+        cols = pl.ds(pl.multiple_of(256 * plane, 256), 256)
+        top = jnp.maximum(
+            jnp.max(scores, axis=1, keepdims=True), jnp.max(self_scores, axis=1, keepdims=True)
+        )
+        weights = jnp.exp(scores - top)
+        self_weight = jnp.exp(self_scores - top)
+        full_total = jnp.sum(weights, axis=1, keepdims=True) + jnp.sum(
+            self_weight, axis=1, keepdims=True
+        )
+        weights = weights.astype(BF16)
+        over = jnp.where(
+            row_of == 0,
+            dot(weights, cache_value[0, :, cols]),
+            dot(weights, cache_value[1, :, cols]),
+        ) + dot(self_weight.astype(BF16), tail_v)
+        heads = jnp.where(key_of == 0, over[:, 0:128], over[:, 128:256]) / full_total
+        send5[pl.ds(pl.multiple_of(32 * plane, 32), 32), :] = heads
+
+    def send_heads(dy):
+        for step in TENSOR_STEPS:
+            if step[0] == dy:
+                peer = tensor_peer(step)
+                remote(
+                    "tensor", peer, send5.at[eight(peer)], recv5.at[eight(me_t)], 4, rsem5.at[me_t]
+                ).start()
+
+    scored = []
+    for dy in PLANE_STEPS:
+        for dz in (0, 1, 3, 2):
+            if dy or dz:
+                peer = tensor_peer((dy, dz))
+                remote(
+                    "tensor", peer, send4.at[peer], recv4.at[peer], 3, rsem4.at[peer]
+                ).wait_recv()
+        scored.append((dy, score(lax.rem(me_y + dy, 4))))
+        if len(scored) > 1:
+            done, parts = scored.pop(0)
+            attend(*parts)
+            send_heads(done)
+    for done, parts in scored:
+        attend(*parts)
+        send_heads(done)
     recv5[eight(me_t), :] = send5[eight(me_t), :]
     sent(0, send1.at[pl.ds(0, GROUPS - 1)])
     sent(1, recv2.at[pl.ds(0, SPLIT - 1)])
@@ -447,7 +459,7 @@
     dma = pltpu.SemaphoreType.DMA
     return pl.pallas_call(
         kernel,
-        out_shape=jax.ShapeDtypeStruct((ROWS, COLS), BF16),
+        out_shape=pltpu.VMEM((ROWS, COLS), BF16),
         in_specs=[large] * 14,
         out_specs=pl.BlockSpec(memory_space=pltpu.VMEM),
         scratch_shapes=[

time: 43 us -> 41 us (0.953)
  Pallas kernels: 41.4 us -> 40.2 us
  local copies, waits for them, and re-layouts: 1.38 us -> 0.62 us
    pallas_call x1, Pallas kernels: 41.4 us -> 40.2 us  [on_device(): pl.pallas_call(kernel, out_shape=pltpu.VMEM((ROWS, COLS), BF16), in_specs...]
    unnamed x1, local copies, waits for them, and re-layouts: 1.38 us -> 0.62 us
where the time goes in v3:
time: 41 us; the launch traced here: 40.9 us
  Pallas kernels  40.2 us (98%)
  local copies, waits for them, and re-layouts  0.62 us (2%)
    pallas_call x1, Pallas kernels, on_device(): pl.pallas_call(kernel, out_shape=pltpu.VMEM((ROWS, COLS), BF16), in_specs...  40.2 us

profile of v3, /device:TPU:0, one launch (start us, length us, event | category | flops | bytes accessed | tf_op | source)
XLA Modules:
  0.0 40.9 jit_solution(9401203713903772668)
XLA Ops:
  0.0 40.2 %shard_map.136 = bf16[32,512]{1,0:T(8,128)(2,1)S(1)} custom-call(s32[1,32]{1,0:T(1,128)} %bitcast.7, s32[1,32]{1,0:T(1,128)} %bitcast.8, s32[1,32]{1,0:T(1,128)} %bitcast.9, bf16[32,8192]{1,0:T(8,128)(2,1)} %tokens_hbm.1, bf16[8192,512]{1,0:T(8,128)(2,1)} %query_hbm.1, bf16[64,8192]{1,0:T(8,128)(2,1)} %bitcast.5, bf16[64,8192]{1,0:T(8,128)(2,1)} %bitcast.6, ...), custom_call_target="tpu_custom_call" | custom-call | tf_op jit(solution)/shard_map/pallas_call | solution.py:460
  40.3 0.6 %copy.16 = bf16[32,512]{1,0:T(8,128)(2,1)} copy(bf16[32,512]{1,0:T(8,128)(2,1)S(1)} %shard_map.136) | data formatting | bytes 65536

commit v4 on v3

--- a/solution.py
+++ b/solution.py
@@ -93,6 +93,7 @@
     recv6,
     local_sem,
     query_sem,
+    plane_sem,
     send_sem,
     rsem1,
     rsem2,
@@ -116,8 +117,11 @@
     batch_peers = [batch_peer(step) for step in BATCH_STEPS]
     tensor_peers = [tensor_peer(step) for step in TENSOR_STEPS]
 
+    ring_z = [tensor_peer((0, step)) for step in (2, 1, 3)]
+    ring_y = [tensor_peer((step, 0)) for step in (2, 1, 3)]
+
     barrier = pltpu.get_barrier_semaphore()
-    for peer in tensor_peers:
+    for peer in ring_z + ring_y:
         pl.semaphore_signal(barrier, inc=1, device_id={"tensor": peer}, device_id_type=MESH)
     for peer in batch_peers:
         pl.semaphore_signal(barrier, inc=1, device_id={"batch": peer}, device_id_type=MESH)
@@ -206,7 +210,9 @@
     )
     send1[:, :, 256:384] = routed_hot.astype(BF16).reshape(GROUPS, 16, 128)
 
-    pl.semaphore_wait(barrier, GROUPS - 1 + SPLIT - 1)
+    pl.semaphore_wait(barrier, GROUPS - 1 + 6)
+    for peer in ring_y:
+        pl.semaphore_signal(plane_sem, inc=1, device_id={"tensor": peer}, device_id_type=MESH)
 
     def remote(axis, peer, source, target, phase, rsem):
         return pltpu.make_async_remote_copy(
@@ -282,6 +288,7 @@
     shrunk = shrunk + pltpu.roll(shrunk, 64, 1)
     send2[...] = jnp.where(iota((32, 128), 1) < 64, shrunk[0:32], shrunk[32:64]).astype(BF16)
 
+    pl.semaphore_wait(plane_sem, 3)
     for peer in tensor_peers:
         remote("tensor", peer, send2, recv2.at[me_t], 1, rsem2.at[me_t]).start()
 
@@ -493,6 +500,7 @@
             pltpu.VMEM((SPLIT, ROWS, COLS), BF16),
             dma((20,)),
             dma((QUERY_CHUNKS,)),
+            pltpu.SemaphoreType.REGULAR,
             dma((6,)),
             dma((GROUPS,)),
             dma((SPLIT,)),

time: 41 us -> 40.3 us (0.983)
  Pallas kernels: 40.2 us -> 39.6 us
    pallas_call x1, Pallas kernels: 40.2 us -> 39.6 us  [on_device(): pl.pallas_call(kernel, out_shape=pltpu.VMEM((ROWS, COLS), BF16), in_specs...]
where the time goes in v4:
time: 40.3 us; the launch traced here: 40.2 us
  Pallas kernels  39.6 us (98%)
  local copies, waits for them, and re-layouts  0.62 us (2%)
    pallas_call x1, Pallas kernels, on_device(): pl.pallas_call(kernel, out_shape=pltpu.VMEM((ROWS, COLS), BF16), in_specs...  39.6 us

profile of v4, /device:TPU:0, one launch (start us, length us, event | category | flops | bytes accessed | tf_op | source)
XLA Modules:
  0.0 40.2 jit_solution(4095769272650750873)
XLA Ops:
  0.0 39.6 %shard_map.136 = bf16[32,512]{1,0:T(8,128)(2,1)S(1)} custom-call(s32[1,32]{1,0:T(1,128)} %bitcast.7, s32[1,32]{1,0:T(1,128)} %bitcast.8, s32[1,32]{1,0:T(1,128)} %bitcast.9, bf16[32,8192]{1,0:T(8,128)(2,1)} %tokens_hbm.1, bf16[8192,512]{1,0:T(8,128)(2,1)} %query_hbm.1, bf16[64,8192]{1,0:T(8,128)(2,1)} %bitcast.5, bf16[64,8192]{1,0:T(8,128)(2,1)} %bitcast.6, ...), custom_call_target="tpu_custom_call" | custom-call | tf_op jit(solution)/shard_map/pallas_call | solution.py:467
  39.6 0.6 %copy.16 = bf16[32,512]{1,0:T(8,128)(2,1)} copy(bf16[32,512]{1,0:T(8,128)(2,1)S(1)} %shard_map.136) | data formatting | bytes 65536

commit v5 on v4

--- a/solution.py
+++ b/solution.py
@@ -43,7 +43,7 @@
 
 
 TENSOR_STEPS = far_first(SPLIT)
-PLANE_STEPS = (0, 1, 3, 2)
+PLANE_STEPS = (0, 3, 1, 2)
 BATCH_STEPS = [(2, 1), (2, 0), (1, 1), (3, 1), (1, 0), (3, 0), (0, 1)]
 
 
@@ -121,10 +121,10 @@
     ring_y = [tensor_peer((step, 0)) for step in (2, 1, 3)]
 
     barrier = pltpu.get_barrier_semaphore()
+    for peer in batch_peers:
+        pl.semaphore_signal(barrier, inc=1, device_id={"batch": peer}, device_id_type=MESH)
     for peer in ring_z + ring_y:
         pl.semaphore_signal(barrier, inc=1, device_id={"tensor": peer}, device_id_type=MESH)
-    for peer in batch_peers:
-        pl.semaphore_signal(barrier, inc=1, device_id={"batch": peer}, device_id_type=MESH)
 
     pending = []
 

time: 40.3 us -> 40.2 us (level)
  no operation moved by 1% of the time
where the time goes in v5:
time: 40.2 us; the launch traced here: 40.1 us
  Pallas kernels  39.5 us (98%)
  local copies, waits for them, and re-layouts  0.62 us (2%)
    pallas_call x1, Pallas kernels, on_device(): pl.pallas_call(kernel, out_shape=pltpu.VMEM((ROWS, COLS), BF16), in_specs...  39.5 us

profile of v5, /device:TPU:0, one launch (start us, length us, event | category | flops | bytes accessed | tf_op | source)
XLA Modules:
  0.0 40.1 jit_solution(15782880020682975905)
XLA Ops:
  0.0 39.5 %shard_map.136 = bf16[32,512]{1,0:T(8,128)(2,1)S(1)} custom-call(s32[1,32]{1,0:T(1,128)} %bitcast.7, s32[1,32]{1,0:T(1,128)} %bitcast.8, s32[1,32]{1,0:T(1,128)} %bitcast.9, bf16[32,8192]{1,0:T(8,128)(2,1)} %tokens_hbm.1, bf16[8192,512]{1,0:T(8,128)(2,1)} %query_hbm.1, bf16[64,8192]{1,0:T(8,128)(2,1)} %bitcast.5, bf16[64,8192]{1,0:T(8,128)(2,1)} %bitcast.6, ...), custom_call_target="tpu_custom_call" | custom-call | tf_op jit(solution)/shard_map/pallas_call | solution.py:467
  39.5 0.6 %copy.16 = bf16[32,512]{1,0:T(8,128)(2,1)} copy(bf16[32,512]{1,0:T(8,128)(2,1)S(1)} %shard_map.136) | data formatting | bytes 65536

commit v6 on v5

--- a/solution.py
+++ b/solution.py
@@ -432,12 +432,13 @@
         [recv5[pl.ds(j, ROWS, stride=4), :].astype(BF16) for j in range(4)], axis=1
     )
 
-    for peer in tensor_peers:
+    sum_steps = [(1, 2), (3, 2), (0, 2), (2, 2), (2, 1), (2, 3), (2, 0), (1, 1), (3, 3), (1, 3), (3, 1), (1, 0), (3, 0), (0, 1), (0, 3)]
+    for peer in [tensor_peer(step) for step in sum_steps]:
         cols = pl.ds(pl.multiple_of(peer * COLS, COLS), COLS)
         send6[peer] = dot(heads, output_w[:, cols]).astype(BF16)
         remote("tensor", peer, send6.at[peer], recv6.at[me_t], 5, rsem6.at[me_t]).start()
     total = dot(heads, output_w[:, own_cols])
-    for dy, dz in TENSOR_STEPS:
+    for dy, dz in sum_steps:
         peer = tensor_peer((4 - dy, 4 - dz))
         remote("tensor", peer, send6.at[peer], recv6.at[peer], 5, rsem6.at[peer]).wait_recv()
         total = total + recv6[peer].astype(F32)

time: 40.2 us -> 40 us (level)
  no operation moved by 1% of the time
where the time goes in v6:
time: 40 us; the launch traced here: 39.9 us
  Pallas kernels  39.3 us (98%)
  local copies, waits for them, and re-layouts  0.62 us (2%)
    pallas_call x1, Pallas kernels, on_device(): pl.pallas_call(kernel, out_shape=pltpu.VMEM((ROWS, COLS), BF16), in_specs...  39.3 us

profile of v6, /device:TPU:0, one launch (start us, length us, event | category | flops | bytes accessed | tf_op | source)
XLA Modules:
  0.0 39.9 jit_solution(1234484708158970858)
XLA Ops:
  0.0 39.3 %shard_map.136 = bf16[32,512]{1,0:T(8,128)(2,1)S(1)} custom-call(s32[1,32]{1,0:T(1,128)} %bitcast.7, s32[1,32]{1,0:T(1,128)} %bitcast.8, s32[1,32]{1,0:T(1,128)} %bitcast.9, bf16[32,8192]{1,0:T(8,128)(2,1)} %tokens_hbm.1, bf16[8192,512]{1,0:T(8,128)(2,1)} %query_hbm.1, bf16[64,8192]{1,0:T(8,128)(2,1)} %bitcast.5, bf16[64,8192]{1,0:T(8,128)(2,1)} %bitcast.6, ...), custom_call_target="tpu_custom_call" | custom-call | tf_op jit(solution)/shard_map/pallas_call | solution.py:468
  39.3 0.6 %copy.16 = bf16[32,512]{1,0:T(8,128)(2,1)} copy(bf16[32,512]{1,0:T(8,128)(2,1)S(1)} %shard_map.136) | data formatting | bytes 65536
